TPU v7x, 32 devices: a whole 2x2x4 slice. The times are simulated.
32 devices in a mesh: space: 8 (over z, y), tensor: 4 (over x, core).
Axes of the slice: x: 2, y: 2, z: 4, core: 2. Of those that a mesh axis runs over, the one named last changes fastest.
Arguments:
- features: bfloat16 [32, 128, 1024], P('space', None, 'tensor'), may hold values from -6 to 6
- depth_kernel: bfloat16 [2, 7, 7, 1024], P(None, None, None, 'tensor'), may hold values from -5 to 5
- norm_gain: float32 [2, 1024], replicated, may hold values from 0.5 to 1.5
- norm_bias: float32 [2, 1024], replicated, may hold values from -3 to 3
- w_expand: bfloat16 [2, 1024, 4096], P(None, None, 'tensor'), may hold values from -0.1875 to 0.1875
- b_expand: float32 [2, 4096], P(None, 'tensor'), may hold values from -3 to 3
- w_reduce: bfloat16 [2, 4096, 1024], P(None, 'tensor'), may hold values from -0.125 to 0.125
- b_reduce: float32 [2, 1024], P(None, 'tensor'), may hold values from -3 to 3
- layer_scale: float32 [2, 1024], P(None, 'tensor'), may hold values from 0.5 to 1.5
Outputs:
- output: bfloat16 [32, 128, 1024], P('space', None, 'tensor')
All inputs are finite; a program needn't handle non-finite values.
Results may differ from a plain program's by a relative error of at most 0.023.
Values may be sent and summed in bfloat16 or wider, within the bound.
A program may use at most 64 MiB of HBM per device.

v0:
```python
import functools

import jax
import jax.numpy as jnp
from jax import lax
from jax.experimental import pallas as pl
from jax.experimental.pallas import tpu as pltpu
from jax.sharding import PartitionSpec as P

D = 1024
TAPS = 7
BLOCKS = 2


def with_halo(x, sides, width):
    for axis, dim in sides:
        devices, length = (lax.axis_size(axis), x.shape[dim])
        up = [(i, (i + 1) % devices) for i in range(devices - 1)]
        down = [(j, i) for i, j in up]
        last = lax.slice_in_dim(x, length - width, length, axis=dim)
        leading = lax.slice_in_dim(x, 0, width, axis=dim)
        before = lax.ppermute(last, axis, up)
        after = lax.ppermute(leading, axis, down)
        x = jnp.concatenate([before, x, after], axis=dim)
    return x


def one_block(stream, kernel, gain, bias, expand, bias_expand, reduce_w, bias_reduce, scale):
    half = TAPS // 2
    height, width, share = stream.shape
    positions = height * width
    padded = with_halo(stream, (("space", 0),), half)
    padded = jnp.pad(padded.astype(jnp.float32), ((0, 0), (half, half), (0, 0)))
    filtered = jnp.zeros(stream.shape, jnp.float32)
    for row_tap in range(TAPS):
        for col_tap in range(TAPS):
            filtered = filtered + padded[
                row_tap : row_tap + height, col_tap : col_tap + width
            ] * kernel[row_tap, col_tap].astype(jnp.float32)
    filtered = filtered.reshape(positions, share)
    offset = lax.axis_index("tensor") * share
    gain_part = lax.dynamic_slice_in_dim(gain, offset, share, 0)
    bias_part = lax.dynamic_slice_in_dim(bias, offset, share, 0)
    sums, squares = lax.psum(
        (jnp.sum(filtered, axis=-1), jnp.sum(filtered * filtered, axis=-1)), "tensor"
    )
    mean = (sums / D)[:, None]
    var = jnp.maximum(squares[:, None] / D - mean * mean, 0.0)
    normed_part = ((filtered - mean) / jnp.sqrt(var + 1e-06) * gain_part + bias_part).astype(
        jnp.bfloat16
    )
    preact = jnp.dot(
        lax.all_gather(normed_part, "tensor", axis=1, tiled=True),
        expand,
        preferred_element_type=jnp.float32,
    )
    hidden = jax.nn.gelu(preact + bias_expand, approximate=False).astype(jnp.bfloat16)
    partial_value = jnp.dot(hidden, reduce_w, preferred_element_type=jnp.float32)
    mixed = lax.psum_scatter(
        partial_value.astype(jnp.bfloat16), "tensor", scatter_dimension=1, tiled=True
    ).astype(jnp.float32)
    updated = stream.reshape(positions, share).astype(jnp.float32) + scale * (mixed + bias_reduce)
    return updated.astype(jnp.bfloat16).reshape(height, width, share)


def per_device(
    features,
    depth_kernel,
    norm_gain,
    norm_bias,
    w_expand,
    b_expand,
    w_reduce,
    b_reduce,
    layer_scale,
):
    stream = features
    for block_id in range(BLOCKS):
        stream = one_block(
            stream,
            depth_kernel[block_id],
            norm_gain[block_id],
            norm_bias[block_id],
            w_expand[block_id],
            b_expand[block_id],
            w_reduce[block_id],
            b_reduce[block_id],
            layer_scale[block_id],
        )
    return stream


MESH = pl.DeviceIdType.MESH
CORES = 4
EXTRA = 16


def shift_down(x, first):
    return jnp.where(first, 0.0, pltpu.roll(x, 1, 0))


def shift_up(x, last):
    return jnp.where(last, 0.0, pltpu.roll(x, x.shape[0] - 1, 0))


def blocks_kernel(
    n_space, feat_in, taps_in, gain_in, nbias_in, w1_in, b1_in, w2_in, b2_in, scale_in, out,
    feat, taps, gain, nbias, w1, b1, w2, b2, scale, taps32, xf, filt, mid, halo, gathered, normed, hidden,
    pair_out, pair_in, cross_out, cross_in, own,
    w_sem, in_sem, halo_send, halo_recv, ag_send, ag_recv, pair_send, pair_recv, cross_send, cross_recv,
):
    rows, width, share = feat.shape
    half = TAPS // 2
    blocks = w1.shape[0]
    band = lax.axis_index("space")
    me = lax.axis_index("tensor")
    core = lax.rem(me, 2)
    mate = me + 1 - 2 * core
    across = lax.rem(me + 2, CORES)
    diagonal = lax.rem(mate + 2, CORES)
    has_up = band > 0
    has_down = band < n_space - 1

    def weight_copies(b):
        return (
            pltpu.make_async_copy(w1_in.at[b], w1.at[b], w_sem.at[b, 0]),
            pltpu.make_async_copy(w2_in.at[b], w2.at[b], w_sem.at[b, 1]),
        )

    pairs_in = (
        (feat_in, feat), (taps_in, taps), (gain_in, gain), (nbias_in, nbias),
        (b1_in, b1), (b2_in, b2), (scale_in, scale),
    )
    small_copies = [
        pltpu.make_async_copy(src, dst, in_sem.at[i]) for i, (src, dst) in enumerate(pairs_in)
    ]
    for copy in small_copies:
        copy.start()
    for b in range(blocks):
        for copy in weight_copies(b):
            copy.start()

    barrier = pltpu.get_barrier_semaphore()
    for who in (mate, across):
        pl.semaphore_signal(barrier, inc=1, device_id=(band, who), device_id_type=MESH)

    @pl.when(has_up)
    def _():
        pl.semaphore_signal(barrier, inc=1, device_id=(band - 1, me), device_id_type=MESH)

    @pl.when(has_down)
    def _():
        pl.semaphore_signal(barrier, inc=1, device_id=(band + 1, me), device_id_type=MESH)

    pl.semaphore_wait(barrier, 2 + jnp.minimum(band, 1) + jnp.minimum(n_space - 1 - band, 1))

    def remote(src, dst, send, recv, who):
        return pltpu.make_async_remote_copy(
            src_ref=src, dst_ref=dst, send_sem=send, recv_sem=recv, device_id=who, device_id_type=MESH
        )

    def halo_copy(b, source, side, i):
        row = i if side == 0 else rows - half + i
        target = (band - 1, me) if side == 0 else (band + 1, me)
        return remote(
            source.at[row], halo.at[b, side, i], halo_send.at[b, side, i], halo_recv.at[b, side, i], target
        )

    present = (has_up, has_down)

    def ag_copy(b, r, kind):
        slot, target = ((me, mate), (me, across), (across, mate))[kind]
        ref = gathered.at[b, r, slot]
        return remote(ref, ref, ag_send.at[b, r, kind], ag_recv.at[b, r, kind], (band, target))

    def pair_copy(b, r):
        return remote(
            pair_out.at[b, r], pair_in.at[b, r], pair_send.at[b, r], pair_recv.at[b, r], (band, mate)
        )

    def cross_copy(b, r):
        return remote(
            cross_out.at[b, r], cross_in.at[b, r], cross_send.at[b, r], cross_recv.at[b, r], (band, across)
        )

    column = lax.broadcasted_iota(jnp.int32, (width, 128), 0)
    lane = lax.broadcasted_iota(jnp.int32, (width, 128), 1)
    first, last, diag = column == 0, column == width - 1, column == lane

    def convolve(b, r, pairs):
        def part(h, fresh):
            ch = pl.ds(pl.multiple_of(h * 128, 128), 128)

            def along(j):
                total = None
                for row, tap in pairs:
                    term = xf[row, :, ch] * taps32[b, tap, pl.ds(j, 1), ch]
                    total = term if total is None else total + term
                return total

            right = shift_down(along(0), first)
            for j in range(1, half):
                right = shift_down(right + along(j), first)
            left = shift_up(along(TAPS - 1), last)
            for j in range(TAPS - 2, half, -1):
                left = shift_up(left + along(j), last)
            total = along(half) + right + left
            if not fresh:
                total = total + filt[r, :, ch]
            filt[r, :, ch] = total

        return part

    def conv_own(b):
        def body(step, carry):
            r, h = step // (share // 128), lax.rem(step, share // 128)
            convolve(b, r, [(half + m, half + m - r) for m in range(rows)])(h, True)
            return carry

        lax.fori_loop(0, rows * (share // 128), body, 0)

    def conv_halo(b, r):
        pairs = []
        for m in range(half):
            row = r + m + rows * ((r + m) // half)
            pairs.append((row, row - r))

        def body(h, carry):
            convolve(b, r, pairs)(h, False)
            return carry

        lax.fori_loop(0, share // 128, body, 0)

    def take_halo(b, upper):
        side, base, there = (1, 0, has_up) if upper else (0, half + rows, has_down)

        @pl.when(there)
        def _():
            for i in range(half):
                halo_copy(b, mid, side, i).wait_recv()
            xf[pl.ds(base, half)] = halo[b, side].astype(jnp.float32)

        @pl.when(jnp.logical_not(there))
        def _():
            xf[pl.ds(base, half)] = jnp.zeros((half, width, share), jnp.float32)

    def send_filtered(b, r):
        value = filt[r]
        center = jnp.sum(value, axis=1, keepdims=True) / share
        gathered[b, r, me, pl.ds(0, width), :] = (value - center).astype(jnp.bfloat16)
        line = jnp.sum(jnp.where(diag, center, 0.0), axis=0, keepdims=True)
        high = line.astype(jnp.bfloat16)
        low = (line - high.astype(jnp.float32)).astype(jnp.bfloat16)
        gathered[b, r, me, pl.ds(width, EXTRA), pl.ds(0, width)] = jnp.broadcast_to(high, (EXTRA, width))
        gathered[b, r, me, pl.ds(width, EXTRA), pl.ds(width, width)] = jnp.broadcast_to(low, (EXTRA, width))
        ag_copy(b, r, 1).start()
        ag_copy(b, r, 0).start()

    def normalize(b, r):
        centers = []
        for s in range(CORES):
            tail = gathered[b, r, s, pl.ds(width, EXTRA), :].astype(jnp.float32)
            line = tail[:1, :width] + tail[:1, width:]
            centers.append(jnp.sum(jnp.where(diag, line, 0.0), axis=1, keepdims=True))
        mean = (centers[0] + centers[1] + centers[2] + centers[3]) / CORES
        deltas = [c - mean for c in centers]
        squares = jnp.zeros((width, 1), jnp.float32)
        for s in range(CORES):
            value = gathered[b, r, s, pl.ds(0, width), :].astype(jnp.float32) + deltas[s]
            squares = squares + jnp.sum(value * value, axis=1, keepdims=True)
        inverse = lax.rsqrt(squares / (share * CORES) + 1e-06)
        for s in range(CORES):
            ch = pl.ds(s * share, share)
            value = gathered[b, r, s, pl.ds(0, width), :].astype(jnp.float32) + deltas[s]
            value = value * inverse * gain[pl.ds(b, 1), ch] + nbias[pl.ds(b, 1), ch]
            normed[:, ch] = value.astype(jnp.bfloat16)

    def expand(b):
        for n in range(w1.shape[2] // 256):
            ch = pl.ds(n * 256, 256)
            x = jnp.dot(normed[...], w1[b, :, ch], preferred_element_type=jnp.float32) + b1[pl.ds(b, 1), ch]
            hidden[:, ch] = (0.5 * x * (1.0 + lax.erf(x * 0.7071067811865476))).astype(jnp.bfloat16)

    def reduce_to(b, owner):
        ch = pl.ds(pl.multiple_of(owner * share, share), share)
        return jnp.dot(hidden[...], w2[b, :, ch], preferred_element_type=jnp.float32)

    def pair_sum(b, r):
        pair_copy(b, r).wait_recv()
        total = cross_out[b, r].astype(jnp.float32) + pair_in[b, r, 1].astype(jnp.float32)
        cross_out[b, r] = total.astype(jnp.bfloat16)
        cross_copy(b, r).start()

    def finish(b, r):
        cross_copy(b, r).wait_recv()
        mixed = own[r] + pair_in[b, r, 0].astype(jnp.float32) + cross_in[b, r].astype(jnp.float32)
        before = (feat if b == 0 else mid)[r].astype(jnp.float32)
        new = (before + scale[pl.ds(b, 1), :] * (mixed + b2[pl.ds(b, 1), :])).astype(jnp.bfloat16)
        if b == blocks - 1:
            out[r] = new
            return
        mid[r] = new
        xf[half + r] = new.astype(jnp.float32)

    def send_halo_row(b, source, r):
        if r < half:
            @pl.when(has_up)
            def _():
                halo_copy(b, source, 0, r).start()
        if r >= rows - half:
            @pl.when(has_down)
            def _():
                halo_copy(b, source, 1, r - (rows - half)).start()

    for r in range(rows):
        send_halo_row(0, feat_in, r)
    for copy in small_copies:
        copy.wait()
    for b in range(blocks):
        taps32[b] = taps[:, :, b, :].astype(jnp.float32)
    for r in range(rows):
        xf[half + r] = feat[r].astype(jnp.float32)

    for b in range(blocks):
        row_of = (lambda k: k) if b == 0 else (lambda k: rows - 1 - k)
        conv_own(b)

        def front(k, carry, b=b, row_of=row_of):
            r = row_of(k)

            @pl.when(k == 0)
            def _():
                take_halo(b, b == 0)

            @pl.when(k == 1)
            def _():
                take_halo(b, b != 0)

            conv_halo(b, r)
            send_filtered(b, r)
            return carry

        lax.fori_loop(0, rows, front, 0)
        for copy in weight_copies(b):
            copy.wait()

        def relay(r, b=b):
            ag_copy(b, r, 1).wait_recv()
            ag_copy(b, r, 2).start()

        relay(row_of(0))

        def middle(k, carry, b=b, row_of=row_of, relay=relay):
            r = row_of(k)
            ag_copy(b, r, 0).wait_recv()
            ag_copy(b, r, 2).wait_recv()
            normalize(b, r)
            expand(b)

            @pl.when(k < rows - 1)
            def _():
                relay(row_of(k + 1))

            @pl.when(k > 0)
            def _():
                pair_sum(b, row_of(k - 1))

            pair_out[b, r, 0] = reduce_to(b, mate).astype(jnp.bfloat16)
            pair_out[b, r, 1] = reduce_to(b, diagonal).astype(jnp.bfloat16)
            pair_copy(b, r).start()
            own[r] = reduce_to(b, me)
            cross_out[b, r] = reduce_to(b, across).astype(jnp.bfloat16)
            return carry

        lax.fori_loop(0, rows, middle, 0)
        pair_sum(b, row_of(rows - 1))
        for k in range(rows):
            finish(b, row_of(k))
            if b < blocks - 1:
                send_halo_row(b + 1, mid, row_of(k))

    for b in range(blocks):
        for side in range(2):
            @pl.when(present[side])
            def _(b=b, side=side):
                for i in range(half):
                    halo_copy(b, feat_in if b == 0 else mid, side, i).wait_send()

        def drain(r, carry, b=b):
            for kind in range(3):
                ag_copy(b, r, kind).wait_send()
            pair_copy(b, r).wait_send()
            cross_copy(b, r).wait_send()
            return carry

        lax.fori_loop(0, rows, drain, 0)


def fused(n_space, features, depth_kernel, gain, nbias, w1, b1, w2, b2, scale):
    rows, width, share = features.shape
    blocks, depth, units = w1.shape
    half = TAPS // 2
    depth_kernel = jnp.transpose(depth_kernel, (1, 2, 0, 3))
    operands = (features, depth_kernel, gain, nbias, w1, b1, w2, b2, scale)
    vmem = pl.BlockSpec(memory_space=pltpu.VMEM)
    hbm = pl.BlockSpec(memory_space=pl.ANY)
    bf, f32 = jnp.bfloat16, jnp.float32
    dma = pltpu.SemaphoreType.DMA
    return pl.pallas_call(
        functools.partial(blocks_kernel, n_space),
        out_shape=jax.ShapeDtypeStruct(features.shape, bf),
        in_specs=[hbm] * len(operands),
        out_specs=vmem,
        scratch_shapes=[
            *[pltpu.VMEM(a.shape, a.dtype) for a in operands],
            pltpu.VMEM((blocks, TAPS, TAPS, share), f32),
            pltpu.VMEM((rows + 2 * half, width, share), f32),
            pltpu.VMEM((rows, width, share), f32),
            pltpu.VMEM((rows, width, share), bf),
            pltpu.VMEM((blocks, 2, half, width, share), bf),
            pltpu.VMEM((blocks, rows, CORES, width + EXTRA, share), bf),
            pltpu.VMEM((width, depth), bf),
            pltpu.VMEM((width, units), bf),
            pltpu.VMEM((blocks, rows, 2, width, share), bf),
            pltpu.VMEM((blocks, rows, 2, width, share), bf),
            pltpu.VMEM((blocks, rows, width, share), bf),
            pltpu.VMEM((blocks, rows, width, share), bf),
            pltpu.VMEM((rows, width, share), f32),
            dma((blocks, 2)),
            dma((7,)),
            dma((blocks, 2, half)),
            dma((blocks, 2, half)),
            dma((blocks, rows, 3)),
            dma((blocks, rows, 3)),
            dma((blocks, rows)),
            dma((blocks, rows)),
            dma((blocks, rows)),
            dma((blocks, rows)),
        ],
        compiler_params=pltpu.CompilerParams(
            collective_id=0, has_side_effects=True, vmem_limit_bytes=64 * 1024 * 1024
        ),
    )(*operands)


def solution(mesh):
    body = per_device
    if mesh.shape["tensor"] == CORES:
        body = functools.partial(fused, mesh.shape["space"])
    return jax.shard_map(
        body,
        mesh=mesh,
        in_specs=(
            P("space", None, "tensor"),
            P(None, None, None, "tensor"),
            P(),
            P(),
            P(None, None, "tensor"),
            P(None, "tensor"),
            P(None, "tensor", None),
            P(None, "tensor"),
            P(None, "tensor"),
        ),
        out_specs=P("space", None, "tensor"),
        check_vma=False,
    )
```

profile of v0, /device:TPU:16, one launch (start us, length us, event | category | flops | bytes accessed | tf_op | source)
XLA Modules:
  0.0 55.1 jit_solution(13645849743030409500)
XLA Ops:
  0.0 53.5 %shard_map.91 = bf16[4,128,256]{2,1,0:T(8,128)(2,1)} custom-call(bf16[4,128,256]{2,1,0:T(8,128)(2,1)} %feat_in.1, bf16[7,7,2,256]{3,2,1,0:T(2,128)(2,1)} %bitcast.1, f32[2,1024]{1,0:T(2,128)} %gain_in.1, f32[2,1024]{1,0:T(2,128)} %nbias_in.1, bf16[2,1024,1024]{2,1,0:T(8,128)(2,1)} %w1_in.1, f32[2,1024]{1,0:T(2,128)} %b1_in.1, bf16[2,1024,1024]{2,1,0:T(8,128)(2,1)} %w2_in.1, ...), custom_call_target="tpu_custom_call" | custom-call | tf_op jit(solution)/shard_map/pallas_call | solution.py:409
  53.5 1.7 %copy.11 = bf16[4,128,256]{2,1,0:T(8,128)(2,1)} copy(bf16[4,128,256]{2,1,0:T(8,128)(2,1)} %shard_map.91) | data formatting | bytes 524288
where the time goes:
time: 55.3 us; the launch traced here: 55.1 us
  Pallas kernels  53.5 us (97%)
  local copies, waits for them, and re-layouts  1.67 us (3%)
    pallas_call x1, Pallas kernels, fused(): pl.pallas_call(functools.partial(blocks_kernel, n_space), out_shape=jax.S...  53.5 us
    unnamed x1, local copies, waits for them, and re-layouts  1.67 us

commit v1 on v0

--- a/solution.py
+++ b/solution.py
@@ -92,7 +92,6 @@
 
 MESH = pl.DeviceIdType.MESH
 CORES = 4
-EXTRA = 16
 
 
 def shift_down(x, first):
@@ -105,7 +104,7 @@
 
 def blocks_kernel(
     n_space, feat_in, taps_in, gain_in, nbias_in, w1_in, b1_in, w2_in, b2_in, scale_in, out,
-    feat, taps, gain, nbias, w1, b1, w2, b2, scale, taps32, xf, filt, mid, halo, gathered, normed, hidden,
+    feat, taps, gain, nbias, w1, b1, w2, b2, scale, taps32, xf, filt, mid, halo, gathered, centers, normed, hidden,
     pair_out, pair_in, cross_out, cross_in, own,
     w_sem, in_sem, halo_send, halo_recv, ag_send, ag_recv, pair_send, pair_recv, cross_send, cross_recv,
 ):
@@ -169,8 +168,8 @@
     present = (has_up, has_down)
 
     def ag_copy(b, r, kind):
-        slot, target = ((me, mate), (me, across), (across, mate))[kind]
-        ref = gathered.at[b, r, slot]
+        slot, target = ((me, mate), (me, across), (across, mate))[kind % 3]
+        ref = (gathered if kind < 3 else centers).at[b, r, slot]
         return remote(ref, ref, ag_send.at[b, r, kind], ag_recv.at[b, r, kind], (band, target))
 
     def pair_copy(b, r):
@@ -231,47 +230,40 @@
 
         lax.fori_loop(0, share // 128, body, 0)
 
-    def take_halo(b, upper):
+    def take_halo(b, upper, i):
         side, base, there = (1, 0, has_up) if upper else (0, half + rows, has_down)
 
         @pl.when(there)
         def _():
-            for i in range(half):
-                halo_copy(b, mid, side, i).wait_recv()
-            xf[pl.ds(base, half)] = halo[b, side].astype(jnp.float32)
+            halo_copy(b, mid, side, i).wait_recv()
+            xf[base + i] = halo[b, side, i].astype(jnp.float32)
 
         @pl.when(jnp.logical_not(there))
         def _():
-            xf[pl.ds(base, half)] = jnp.zeros((half, width, share), jnp.float32)
+            xf[base + i] = jnp.zeros((width, share), jnp.float32)
 
     def send_filtered(b, r):
         value = filt[r]
         center = jnp.sum(value, axis=1, keepdims=True) / share
-        gathered[b, r, me, pl.ds(0, width), :] = (value - center).astype(jnp.bfloat16)
-        line = jnp.sum(jnp.where(diag, center, 0.0), axis=0, keepdims=True)
-        high = line.astype(jnp.bfloat16)
-        low = (line - high.astype(jnp.float32)).astype(jnp.bfloat16)
-        gathered[b, r, me, pl.ds(width, EXTRA), pl.ds(0, width)] = jnp.broadcast_to(high, (EXTRA, width))
-        gathered[b, r, me, pl.ds(width, EXTRA), pl.ds(width, width)] = jnp.broadcast_to(low, (EXTRA, width))
-        ag_copy(b, r, 1).start()
-        ag_copy(b, r, 0).start()
+        gathered[b, r, me] = (value - center).astype(jnp.bfloat16)
+        centers[b, r, me] = jnp.sum(jnp.where(diag, center, 0.0), axis=0, keepdims=True)
+        for kind in (4, 1, 3, 0):
+            ag_copy(b, r, kind).start()
 
     def normalize(b, r):
-        centers = []
-        for s in range(CORES):
-            tail = gathered[b, r, s, pl.ds(width, EXTRA), :].astype(jnp.float32)
-            line = tail[:1, :width] + tail[:1, width:]
-            centers.append(jnp.sum(jnp.where(diag, line, 0.0), axis=1, keepdims=True))
-        mean = (centers[0] + centers[1] + centers[2] + centers[3]) / CORES
-        deltas = [c - mean for c in centers]
+        own_means = [
+            jnp.sum(jnp.where(diag, centers[b, r, s], 0.0), axis=1, keepdims=True) for s in range(CORES)
+        ]
+        mean = (own_means[0] + own_means[1] + own_means[2] + own_means[3]) / CORES
+        deltas = [c - mean for c in own_means]
         squares = jnp.zeros((width, 1), jnp.float32)
         for s in range(CORES):
-            value = gathered[b, r, s, pl.ds(0, width), :].astype(jnp.float32) + deltas[s]
+            value = gathered[b, r, s].astype(jnp.float32) + deltas[s]
             squares = squares + jnp.sum(value * value, axis=1, keepdims=True)
         inverse = lax.rsqrt(squares / (share * CORES) + 1e-06)
         for s in range(CORES):
             ch = pl.ds(s * share, share)
-            value = gathered[b, r, s, pl.ds(0, width), :].astype(jnp.float32) + deltas[s]
+            value = gathered[b, r, s].astype(jnp.float32) + deltas[s]
             value = value * inverse * gain[pl.ds(b, 1), ch] + nbias[pl.ds(b, 1), ch]
             normed[:, ch] = value.astype(jnp.bfloat16)
 
@@ -302,18 +294,13 @@
         mid[r] = new
         xf[half + r] = new.astype(jnp.float32)
 
-    def send_halo_row(b, source, r):
-        if r < half:
-            @pl.when(has_up)
-            def _():
-                halo_copy(b, source, 0, r).start()
-        if r >= rows - half:
-            @pl.when(has_down)
-            def _():
-                halo_copy(b, source, 1, r - (rows - half)).start()
-
-    for r in range(rows):
-        send_halo_row(0, feat_in, r)
+    def send_halo(b, source, side, i):
+        @pl.when(present[side])
+        def _():
+            halo_copy(b, source, side, i).start()
+
+    for i in range(half):
+        send_halo(0, feat_in, 1, i)
     for copy in small_copies:
         copy.wait()
     for b in range(blocks):
@@ -322,38 +309,54 @@
         xf[half + r] = feat[r].astype(jnp.float32)
 
     for b in range(blocks):
-        row_of = (lambda k: k) if b == 0 else (lambda k: rows - 1 - k)
+        downward = b % 2 == 0
+        row_of = (lambda k: k) if downward else (lambda k: rows - 1 - k)
         conv_own(b)
-
-        def front(k, carry, b=b, row_of=row_of):
+        if b == 0:
+            @pl.when(has_down)
+            def _():
+                for i in range(half):
+                    halo_copy(0, feat_in, 1, i).wait_send()
+
+            for i in range(half):
+                send_halo(0, feat_in, 0, i)
+        else:
+            send_halo(b, mid, 1 if not downward else 0, half - 2 if not downward else 1)
+
+        for i in range(half):
+            take_halo(b, downward, i)
+
+        def front(k, carry, b=b, row_of=row_of, downward=downward):
             r = row_of(k)
 
-            @pl.when(k == 0)
+            @pl.when(k > 0)
             def _():
-                take_halo(b, b == 0)
-
-            @pl.when(k == 1)
-            def _():
-                take_halo(b, b != 0)
+                take_halo(b, not downward, k - 1 if downward else rows - 1 - k)
 
             conv_halo(b, r)
             send_filtered(b, r)
             return carry
 
-        lax.fori_loop(0, rows, front, 0)
+        if b > 0:
+            front(0, 0)
+            send_halo(b, mid, 1 if not downward else 0, 0 if not downward else half - 1)
+            lax.fori_loop(1, rows, front, 0)
+        else:
+            lax.fori_loop(0, rows, front, 0)
         for copy in weight_copies(b):
             copy.wait()
 
         def relay(r, b=b):
-            ag_copy(b, r, 1).wait_recv()
-            ag_copy(b, r, 2).start()
+            for kind in (4, 1):
+                ag_copy(b, r, kind).wait_recv()
+                ag_copy(b, r, kind + 1).start()
 
         relay(row_of(0))
 
         def middle(k, carry, b=b, row_of=row_of, relay=relay):
             r = row_of(k)
-            ag_copy(b, r, 0).wait_recv()
-            ag_copy(b, r, 2).wait_recv()
+            for kind in (0, 3, 2, 5):
+                ag_copy(b, r, kind).wait_recv()
             normalize(b, r)
             expand(b)
 
@@ -375,19 +378,29 @@
         lax.fori_loop(0, rows, middle, 0)
         pair_sum(b, row_of(rows - 1))
         for k in range(rows):
-            finish(b, row_of(k))
-            if b < blocks - 1:
-                send_halo_row(b + 1, mid, row_of(k))
+            r = row_of(k)
+            finish(b, r)
+            if b == blocks - 1:
+                continue
+            if downward and r < half:
+                send_halo(b + 1, mid, 0, r)
+            if not downward and r >= rows - half:
+                send_halo(b + 1, mid, 1, r - (rows - half))
+            if k == rows - 1:
+                send_halo(b + 1, mid, 1 if downward else 0, half - 1 if downward else 0)
 
     for b in range(blocks):
         for side in range(2):
+            if b == 0 and side == 1:
+                continue
+
             @pl.when(present[side])
             def _(b=b, side=side):
                 for i in range(half):
                     halo_copy(b, feat_in if b == 0 else mid, side, i).wait_send()
 
         def drain(r, carry, b=b):
-            for kind in range(3):
+            for kind in range(6):
                 ag_copy(b, r, kind).wait_send()
             pair_copy(b, r).wait_send()
             cross_copy(b, r).wait_send()
@@ -418,7 +431,8 @@
             pltpu.VMEM((rows, width, share), f32),
             pltpu.VMEM((rows, width, share), bf),
             pltpu.VMEM((blocks, 2, half, width, share), bf),
-            pltpu.VMEM((blocks, rows, CORES, width + EXTRA, share), bf),
+            pltpu.VMEM((blocks, rows, CORES, width, share), bf),
+            pltpu.VMEM((blocks, rows, CORES, 1, width), f32),
             pltpu.VMEM((width, depth), bf),
             pltpu.VMEM((width, units), bf),
             pltpu.VMEM((blocks, rows, 2, width, share), bf),
@@ -430,8 +444,8 @@
             dma((7,)),
             dma((blocks, 2, half)),
             dma((blocks, 2, half)),
-            dma((blocks, rows, 3)),
-            dma((blocks, rows, 3)),
+            dma((blocks, rows, 6)),
+            dma((blocks, rows, 6)),
             dma((blocks, rows)),
             dma((blocks, rows)),
             dma((blocks, rows)),

time: 55.3 us -> 51.4 us (0.929)
  Pallas kernels: 53.5 us -> 49.4 us
    pallas_call x1, Pallas kernels: 53.5 us -> 49.4 us  [fused(): pl.pallas_call(functools.partial(blocks_kernel, n_space), out_shape=jax.S...]
where the time goes in v1:
time: 51.4 us; the launch traced here: 51.1 us
  Pallas kernels  49.4 us (96%)
  local copies, waits for them, and re-layouts  1.67 us (3%)
    pallas_call x1, Pallas kernels, fused(): pl.pallas_call(functools.partial(blocks_kernel, n_space), out_shape=jax.S...  49.4 us
    unnamed x1, local copies, waits for them, and re-layouts  1.67 us

profile of v1, /device:TPU:16, one launch (start us, length us, event | category | flops | bytes accessed | tf_op | source)
XLA Modules:
  0.0 51.1 jit_solution(8145547561178765642)
XLA Ops:
  0.0 49.4 %shard_map.91 = bf16[4,128,256]{2,1,0:T(8,128)(2,1)} custom-call(bf16[4,128,256]{2,1,0:T(8,128)(2,1)} %feat_in.1, bf16[7,7,2,256]{3,2,1,0:T(2,128)(2,1)} %bitcast.1, f32[2,1024]{1,0:T(2,128)} %gain_in.1, f32[2,1024]{1,0:T(2,128)} %nbias_in.1, bf16[2,1024,1024]{2,1,0:T(8,128)(2,1)} %w1_in.1, f32[2,1024]{1,0:T(2,128)} %b1_in.1, bf16[2,1024,1024]{2,1,0:T(8,128)(2,1)} %w2_in.1, ...), custom_call_target="tpu_custom_call" | custom-call | tf_op jit(solution)/shard_map/pallas_call | solution.py:422
  49.4 1.7 %copy.11 = bf16[4,128,256]{2,1,0:T(8,128)(2,1)} copy(bf16[4,128,256]{2,1,0:T(8,128)(2,1)} %shard_map.91) | data formatting | bytes 524288

commit v2 on v1

--- a/solution.py
+++ b/solution.py
@@ -210,16 +210,21 @@
 
         return part
 
+    def early_rows(b):
+        if b == 0:
+            return range(rows)
+        return range(rows - 1) if b % 2 == 1 else range(1, rows)
+
     def conv_own(b):
         def body(step, carry):
             r, h = step // (share // 128), lax.rem(step, share // 128)
-            convolve(b, r, [(half + m, half + m - r) for m in range(rows)])(h, True)
+            convolve(b, r, [(half + m, half + m - r) for m in early_rows(b)])(h, True)
             return carry
 
         lax.fori_loop(0, rows * (share // 128), body, 0)
 
     def conv_halo(b, r):
-        pairs = []
+        pairs = [(half + m, half + m - r) for m in range(rows) if m not in early_rows(b)]
         for m in range(half):
             row = r + m + rows * ((r + m) // half)
             pairs.append((row, row - r))
@@ -311,8 +316,9 @@
     for b in range(blocks):
         downward = b % 2 == 0
         row_of = (lambda k: k) if downward else (lambda k: rows - 1 - k)
-        conv_own(b)
         if b == 0:
+            conv_own(b)
+
             @pl.when(has_down)
             def _():
                 for i in range(half):
@@ -351,43 +357,63 @@
                 ag_copy(b, r, kind).wait_recv()
                 ag_copy(b, r, kind + 1).start()
 
-        relay(row_of(0))
-
-        def middle(k, carry, b=b, row_of=row_of, relay=relay):
-            r = row_of(k)
+        def arrive(r, b=b):
             for kind in (0, 3, 2, 5):
                 ag_copy(b, r, kind).wait_recv()
-            normalize(b, r)
+
+        def send_partials(r, b=b):
+            pair_out[b, r, 0] = reduce_to(b, mate).astype(jnp.bfloat16)
+            pair_out[b, r, 1] = reduce_to(b, diagonal).astype(jnp.bfloat16)
+            pair_copy(b, r).start()
+
+        def keep_partials(r, b=b):
+            own[r] = reduce_to(b, me)
+            cross_out[b, r] = reduce_to(b, across).astype(jnp.bfloat16)
+
+        def finish_and_send(k, b=b, row_of=row_of, downward=downward):
+            r = row_of(k)
+            finish(b, r)
+            if b < blocks - 1:
+                send_halo(b + 1, mid, 0 if downward else 1, r if downward else r - (rows - half))
+
+        relay(row_of(0))
+        arrive(row_of(0))
+        normalize(b, row_of(0))
+
+        def middle(k, carry, b=b, row_of=row_of):
+            r = row_of(k)
+            after = row_of(k + 1)
             expand(b)
-
-            @pl.when(k < rows - 1)
-            def _():
-                relay(row_of(k + 1))
+            relay(after)
 
             @pl.when(k > 0)
             def _():
                 pair_sum(b, row_of(k - 1))
 
-            pair_out[b, r, 0] = reduce_to(b, mate).astype(jnp.bfloat16)
-            pair_out[b, r, 1] = reduce_to(b, diagonal).astype(jnp.bfloat16)
-            pair_copy(b, r).start()
-            own[r] = reduce_to(b, me)
-            cross_out[b, r] = reduce_to(b, across).astype(jnp.bfloat16)
+            send_partials(r)
+            arrive(after)
+            keep_partials(r)
+            normalize(b, after)
+
+            @pl.when(k > 1)
+            def _():
+                finish_and_send(k - 2)
+
             return carry
 
-        lax.fori_loop(0, rows, middle, 0)
+        lax.fori_loop(0, rows - 1, middle, 0)
+        expand(b)
+        pair_sum(b, row_of(rows - 2))
+        send_partials(row_of(rows - 1))
+        keep_partials(row_of(rows - 1))
+        finish_and_send(rows - 3)
         pair_sum(b, row_of(rows - 1))
-        for k in range(rows):
-            r = row_of(k)
-            finish(b, r)
-            if b == blocks - 1:
-                continue
-            if downward and r < half:
-                send_halo(b + 1, mid, 0, r)
-            if not downward and r >= rows - half:
-                send_halo(b + 1, mid, 1, r - (rows - half))
-            if k == rows - 1:
-                send_halo(b + 1, mid, 1 if downward else 0, half - 1 if downward else 0)
+        finish_and_send(rows - 2)
+        if b < blocks - 1:
+            conv_own(b + 1)
+        finish(b, row_of(rows - 1))
+        if b < blocks - 1:
+            send_halo(b + 1, mid, 1 if downward else 0, half - 1 if downward else 0)
 
     for b in range(blocks):
         for side in range(2):
@@ -458,9 +484,13 @@
 
 
 def solution(mesh):
-    body = per_device
-    if mesh.shape["tensor"] == CORES:
-        body = functools.partial(fused, mesh.shape["space"])
+    sizes = dict(mesh.shape)
+
+    def body(features, *rest):
+        if sizes["tensor"] == CORES and features.shape == (TAPS // 2 + 1, 128, 256):
+            return fused(sizes["space"], features, *rest)
+        return per_device(features, *rest)
+
     return jax.shard_map(
         body,
         mesh=mesh,

time: 51.4 us -> 51.5 us (level)
  no operation moved by 1% of the time
where the time goes in v2:
time: 51.5 us; the launch traced here: 51.4 us
  Pallas kernels  49.7 us (97%)
  local copies, waits for them, and re-layouts  1.67 us (3%)
    pallas_call x1, Pallas kernels, fused(): pl.pallas_call(functools.partial(blocks_kernel, n_space), out_shape=jax.S...  49.7 us
    unnamed x1, local copies, waits for them, and re-layouts  1.67 us

profile of v2, /device:TPU:16, one launch (start us, length us, event | category | flops | bytes accessed | tf_op | source)
XLA Modules:
  0.0 51.4 jit_solution(10118528804546702503)
XLA Ops:
  0.0 49.7 %shard_map.91 = bf16[4,128,256]{2,1,0:T(8,128)(2,1)} custom-call(bf16[4,128,256]{2,1,0:T(8,128)(2,1)} %feat_in.1, bf16[7,7,2,256]{3,2,1,0:T(2,128)(2,1)} %bitcast.1, f32[2,1024]{1,0:T(2,128)} %gain_in.1, f32[2,1024]{1,0:T(2,128)} %nbias_in.1, bf16[2,1024,1024]{2,1,0:T(8,128)(2,1)} %w1_in.1, f32[2,1024]{1,0:T(2,128)} %b1_in.1, bf16[2,1024,1024]{2,1,0:T(8,128)(2,1)} %w2_in.1, ...), custom_call_target="tpu_custom_call" | custom-call | tf_op jit(solution)/shard_map/pallas_call | solution.py:448
  49.7 1.7 %copy.11 = bf16[4,128,256]{2,1,0:T(8,128)(2,1)} copy(bf16[4,128,256]{2,1,0:T(8,128)(2,1)} %shard_map.91) | data formatting | bytes 524288
